TPU v7x, 256 devices: a whole 4x4x8 slice. The times are simulated.
256 devices in a mesh: gx: 8 (over x, core), gyz: 8 (over y, z_lo), band: 4 (over z_hi).
Axes of the slice: x: 4, y: 4, z: 8 (z_hi: 4, z_lo: 2; z = z_hi * 2 + z_lo), core: 2. Of those that a mesh axis runs over, the one named last changes fastest.
Arguments:
- orbitals: float32 [256, 32, 64, 128], P('band', 'gx', 'gyz'), may hold values from -6 to 6
- v_local: float32 [32, 64, 128], P('gx', 'gyz'), may hold values from 0 to 2
- features: bfloat16 [11, 32, 64, 128], P(None, 'gx', 'gyz'), may hold values from -6 to 6
- w_first: bfloat16 [256, 11], replicated, may hold values from -1.75 to 1.75
- w_hidden: bfloat16 [1, 256, 256], replicated, may hold values from -0.375 to 0.375
- w_last: bfloat16 [256], replicated, may hold values from -0.375 to 0.375
- rotation: float32 [256, 256], replicated, may hold values from -0.375 to 0.375
- assignment: int32 [256], replicated, may hold values from 0 to 255, each once
- degrees: int32 [256], P('band'), may hold values from 4 to 8, as said below
Outputs:
- gram: float32 [256, 256], P('band')
- rotated: float32 [256, 32, 64, 128], P('band', 'gx', 'gyz')
Inputs may be any that keep to these rules, and one draw needn't show every extreme that they name: `degrees`: a filter degree of each slot; some slot has 8 and some has 4. `assignment`: each orbital is held in exactly one slot.
All inputs are finite; a program needn't handle non-finite values.
Results may differ from a plain program's by a relative error of at most 0.0043.
Values may be sent and summed in bfloat16 or wider, within the bound.
No kernel may reach another device: no remote copies, remote signals or barrier semaphores. Data moves between devices by JAX's collectives and lax.ppermute only.
A program may use at most 64 MiB of HBM per device.

v0:
```python
import jax
import jax.numpy as jnp
from jax import lax
from jax.sharding import PartitionSpec as P

DEG = 8
LOWER_EDGE = 2.0
CUT_EDGE = 3.0
UPPER_EDGE = 9.5


def with_halo(block, sides, width):
    for axis, dim in sides:
        count = lax.axis_size(axis)
        forward = [(i, i + 1) for i in range(count - 1)]
        backward = [(target, source) for source, target in forward]
        low = lax.ppermute(
            lax.slice_in_dim(block, block.shape[dim] - width, None, axis=dim), axis, forward
        )
        high = lax.ppermute(lax.slice_in_dim(block, 0, width, axis=dim), axis, backward)
        block = jnp.concatenate([low, block, high], axis=dim)
    return block


def coefficients(count):
    half_width = (UPPER_EDGE - CUT_EDGE) / 2.0
    centre = (UPPER_EDGE + CUT_EDGE) / 2.0
    first = half_width / (LOWER_EDGE - centre)
    factors = [(first / half_width, 0.0)]
    sigma = first
    for rounds in range(1, count):
        updated = 1.0 / (2.0 / first - sigma)
        factors.append((2.0 * updated / half_width, sigma * updated))
        sigma = updated
    return (factors, centre)


def hamiltonian(field, potential):
    padded = with_halo(field, (("gx", 1), ("gyz", 2)), 1)
    padded = jnp.pad(padded, ((0, 0), (0, 0), (0, 0), (1, 1)))
    beside_all = padded[:, 2:, 1:-1, 1:-1] + padded[:, :-2, 1:-1, 1:-1]
    beside_all = beside_all + padded[:, 1:-1, 2:, 1:-1] + padded[:, 1:-1, :-2, 1:-1]
    beside_all = beside_all + padded[:, 1:-1, 1:-1, 2:] + padded[:, 1:-1, 1:-1, :-2]
    return 0.5 * (6.0 * field - beside_all) + potential * field


def network(cell_features, w_first, w_hidden, w_last):
    feature_count = cell_features.shape[0]
    flattened = cell_features.reshape(feature_count, -1)
    hidden = jax.nn.silu(jnp.dot(w_first, flattened, preferred_element_type=jnp.float32)).astype(
        jnp.bfloat16
    )
    hidden = jax.nn.silu(jnp.dot(w_hidden[0], hidden, preferred_element_type=jnp.float32)).astype(
        jnp.bfloat16
    )
    values = jnp.tanh(jnp.dot(w_last[None, :], hidden, preferred_element_type=jnp.float32)[0])
    return values.reshape(cell_features.shape[1:])


def on_device(
    orbitals, v_local, features, w_first, w_hidden, w_last, rotation, assignment, degrees
):
    group = lax.axis_index("band")
    local_slots, size_x, size_y, size_z = orbitals.shape
    total_slots = rotation.shape[0]
    cells = size_x * size_y * size_z
    total_cells = float(cells * lax.axis_size("gx") * lax.axis_size("gyz"))
    xc_field = network(features, w_first, w_hidden, w_last)
    potential = v_local + xc_field
    factors, centre = coefficients(DEG)
    previous = orbitals
    current = orbitals
    for rounds in range(DEG):
        image = hamiltonian(current, potential)
        scale_new, scale_old = factors[rounds]
        updated = scale_new * (image - centre * current) - scale_old * previous
        active = (degrees > rounds)[:, None, None, None]
        previous = jnp.where(active, current, previous)
        current = jnp.where(active, updated, current)
    filtered = current.astype(jnp.bfloat16).reshape(local_slots, cells)
    select = (assignment[:, None] == lax.iota(jnp.int32, total_slots)[None, :]).astype(jnp.float32)
    permuted = jnp.dot(select, rotation, precision=lax.Precision.HIGHEST)
    slot_rotation = jnp.dot(permuted, select.T, precision=lax.Precision.HIGHEST).astype(
        jnp.bfloat16
    )
    own_columns = lax.dynamic_slice_in_dim(slot_rotation, group * local_slots, local_slots, 1)
    shard_rows = lax.all_gather(filtered, "band", axis=0, tiled=True)
    margin = lax.dot_general(
        filtered, shard_rows, (((1,), (1,)), ((), ())), preferred_element_type=jnp.float32
    )
    gram_part = margin
    rotated_part = lax.dot_general(
        own_columns, shard_rows, (((0,), (0,)), ((), ())), preferred_element_type=jnp.float32
    )
    gram_part, rotated_flat = (gram_part, rotated_part)
    gram = lax.psum(gram_part, ("gx", "gyz")) / total_cells
    rotated = rotated_flat.reshape(local_slots, size_x, size_y, size_z)
    return (gram, rotated)


def solution(mesh):
    placed = (
        P("band", "gx", "gyz", None),
        P("gx", "gyz", None),
        P(None, "gx", "gyz", None),
        P(),
        P(),
        P(),
        P(),
        P(),
        P("band"),
    )
    return jax.shard_map(
        on_device,
        mesh=mesh,
        in_specs=placed,
        out_specs=(P("band", None), P("band", "gx", "gyz", None)),
        check_vma=False,
    )
```

profile of v0, /device:TPU:8, one launch (start us, length us, event | category | flops | bytes accessed | tf_op | source)
XLA Modules:
  0.0 750.5 jit_solution(973591448265603997)
XLA Ops:
  21.3 3.7 collective-permute-start.2
  29.3 6.6 collective-permute-done.3
  45.5 3.8 collective-permute-start.7
  51.0 3.5 collective-permute-done.7
  59.2 4.8 collective-permute-start.9
  67.1 3.9 collective-permute-start.11
  72.7 4.7 collective-permute-done.11
  82.6 5.3 collective-permute-start.13
  91.0 4.1 collective-permute-start.15
  96.6 4.7 collective-permute-done.15
  106.7 5.3 collective-permute-start.17
  115.0 3.9 collective-permute-start.19
  120.7 4.7 collective-permute-done.19
  130.1 5.3 collective-permute-start.21
  138.5 3.9 collective-permute-start.23
  144.2 4.7 collective-permute-done.23
  154.0 5.3 collective-permute-start.25
  162.3 3.9 collective-permute-start.27
  168.0 4.7 collective-permute-done.27
  177.4 5.3 collective-permute-start.29
  185.8 3.9 collective-permute-start.31
  191.4 4.7 collective-permute-done.31
  201.8 60.9 %all-gather.2.cloned.1.call-done = bf16[256,4096]{1,0:T(8,128)(2,1)} async-done(((bf16[64,4096]{1,0:T(8,128)(2,1)}), bf16[256,4096]{1,0:T(8,128)(2,1)}) %all-gather.2.cloned.1.call-update) | async-done | bytes 2097168 | tf_op jit(solution)/shard_map/all_gather | solution.py:87
  267.6 474.6 %all-reduce.10.cloned.1.call-done = f32[64,256]{1,0:T(8,128)} async-done(((f32[64,256]{1,0:T(8,128)}), f32[64,256]{1,0:T(8,128)}) %all-reduce.10.cloned.1.call-update) | async-done | bytes 65552 | tf_op jit(solution)/shard_map/psum | solution.py:96
  (109 shorter events, 99.3 us)
Async XLA Ops:
  7.2 255.5 %all-gather.2.cloned.1.call-start = ((), (), s32[]{:S(2)}) async-start(), calls=%async_computation | async-start | bytes 2621440 | tf_op jit(solution)/shard_map/all_gather | solution.py:87
  9.1 11.5 %collective-permute-start.1 = (f32[64,1,8,128]{3,0,2,1:T(8,128)S(1)}, f32[64,1,8,128]{3,0,2,1:T(8,128)S(1)}, u32[]{:S(2)}, u32[]{:S(2)}) collective-permute-start(f32[64,1,8,128]{3,0,2,1:T(8,128)S(1)} %get-tuple-element.37), channel_id=1, source_target_pairs={{0,32},{32,64},{64,96},{96,128},{128,160},{160,192},{192,224},{1,3... | collective-permute-start | bytes 786440 | tf_op jit(solution)/shard_map/ppermute | solution.py:17
  10.9 10.4 %collective-permute-start = (f32[64,1,8,128]{3,0,2,1:T(8,128)S(1)}, f32[64,1,8,128]{3,0,2,1:T(8,128)S(1)}, u32[]{:S(2)}, u32[]{:S(2)}) collective-permute-start(f32[64,1,8,128]{3,0,2,1:T(8,128)S(1)} %get-tuple-element.36), channel_id=1, source_target_pairs={{32,0},{64,32},{96,64},{128,96},{160,128},{192,160},{224,192},{33,... | collective-permute-start | bytes 786440 | tf_op jit(solution)/shard_map/ppermute | solution.py:20
  21.3 8.0 %collective-permute-start.2 = (f32[64,6,1,128]{3,0,2,1:T(8,128)S(1)}, f32[64,6,1,128]{3,0,2,1:T(8,128)S(1)}, u32[]{:S(2)}, u32[]{:S(2)}) collective-permute-start(f32[64,6,1,128]{3,0,2,1:T(8,128)S(1)} %get-tuple-element.21), channel_id=1, source_target_pairs={{4,0},{8,4},{12,8},{16,12},{20,16},{24,20},{28,24},{5,1},{9,5},{13... | collective-permute-start | bytes 589832 | tf_op jit(solution)/shard_map/ppermute | solution.py:20
  25.1 10.9 %collective-permute-start.3 = (f32[64,6,1,128]{3,0,2,1:T(8,128)S(1)}, f32[64,6,1,128]{3,0,2,1:T(8,128)S(1)}, u32[]{:S(2)}, u32[]{:S(2)}) collective-permute-start(f32[64,6,1,128]{3,0,2,1:T(8,128)S(1)} %get-tuple-element.20), channel_id=1, source_target_pairs={{0,4},{4,8},{8,12},{12,16},{16,20},{20,24},{24,28},{1,5},{5,9},{9,... | collective-permute-start | bytes 589832 | tf_op jit(solution)/shard_map/ppermute | solution.py:17
  43.4 7.6 %collective-permute-start.6 = (f32[64,6,1,128]{3,0,2,1:T(8,128)S(1)}, f32[64,6,1,128]{3,0,2,1:T(8,128)S(1)}, u32[]{:S(2)}, u32[]{:S(2)}) collective-permute-start(f32[64,6,1,128]{3,0,2,1:T(8,128)S(1)} %get-tuple-element.19), channel_id=1, source_target_pairs={{4,0},{8,4},{12,8},{16,12},{20,16},{24,20},{28,24},{5,1},{9,5},{13... | collective-permute-start | bytes 589832 | tf_op jit(solution)/shard_map/ppermute | solution.py:20
  45.5 9.0 %collective-permute-start.7 = (f32[64,6,1,128]{3,0,2,1:T(8,128)S(1)}, f32[64,6,1,128]{3,0,2,1:T(8,128)S(1)}, u32[]{:S(2)}, u32[]{:S(2)}) collective-permute-start(f32[64,6,1,128]{3,0,2,1:T(8,128)S(1)} %get-tuple-element.18), channel_id=1, source_target_pairs={{0,4},{4,8},{8,12},{12,16},{16,20},{20,24},{24,28},{1,5},{5,9},{9,... | collective-permute-start | bytes 589832 | tf_op jit(solution)/shard_map/ppermute | solution.py:17
  65.1 7.6 %collective-permute-start.10 = (f32[64,6,1,128]{3,0,2,1:T(8,128)S(1)}, f32[64,6,1,128]{3,0,2,1:T(8,128)S(1)}, u32[]{:S(2)}, u32[]{:S(2)}) collective-permute-start(f32[64,6,1,128]{3,0,2,1:T(8,128)S(1)} %get-tuple-element.17), channel_id=1, source_target_pairs={{4,0},{8,4},{12,8},{16,12},{20,16},{24,20},{28,24},{5,1},{9,5},{13... | collective-permute-start | bytes 589832 | tf_op jit(solution)/shard_map/ppermute | solution.py:20
  67.1 10.4 %collective-permute-start.11 = (f32[64,6,1,128]{3,0,2,1:T(8,128)S(1)}, f32[64,6,1,128]{3,0,2,1:T(8,128)S(1)}, u32[]{:S(2)}, u32[]{:S(2)}) collective-permute-start(f32[64,6,1,128]{3,0,2,1:T(8,128)S(1)} %get-tuple-element.16), channel_id=1, source_target_pairs={{0,4},{4,8},{8,12},{12,16},{16,20},{20,24},{24,28},{1,5},{5,9},{9,... | collective-permute-start | bytes 589832 | tf_op jit(solution)/shard_map/ppermute | solution.py:17
  81.3 6.6 collective-permute-start.12
  89.0 7.6 %collective-permute-start.14 = (f32[64,6,1,128]{3,0,2,1:T(8,128)S(1)}, f32[64,6,1,128]{3,0,2,1:T(8,128)S(1)}, u32[]{:S(2)}, u32[]{:S(2)}) collective-permute-start(f32[64,6,1,128]{3,0,2,1:T(8,128)S(1)} %get-tuple-element.15), channel_id=1, source_target_pairs={{4,0},{8,4},{12,8},{16,12},{20,16},{24,20},{28,24},{5,1},{9,5},{13... | collective-permute-start | bytes 589832 | tf_op jit(solution)/shard_map/ppermute | solution.py:20
  91.0 10.4 %collective-permute-start.15 = (f32[64,6,1,128]{3,0,2,1:T(8,128)S(1)}, f32[64,6,1,128]{3,0,2,1:T(8,128)S(1)}, u32[]{:S(2)}, u32[]{:S(2)}) collective-permute-start(f32[64,6,1,128]{3,0,2,1:T(8,128)S(1)} %get-tuple-element.14), channel_id=1, source_target_pairs={{0,4},{4,8},{8,12},{12,16},{16,20},{20,24},{24,28},{1,5},{5,9},{9,... | collective-permute-start | bytes 589832 | tf_op jit(solution)/shard_map/ppermute | solution.py:17
  113.1 7.6 %collective-permute-start.18 = (f32[64,6,1,128]{3,0,2,1:T(8,128)S(1)}, f32[64,6,1,128]{3,0,2,1:T(8,128)S(1)}, u32[]{:S(2)}, u32[]{:S(2)}) collective-permute-start(f32[64,6,1,128]{3,0,2,1:T(8,128)S(1)} %get-tuple-element.13), channel_id=1, source_target_pairs={{4,0},{8,4},{12,8},{16,12},{20,16},{24,20},{28,24},{5,1},{9,5},{13... | collective-permute-start | bytes 589832 | tf_op jit(solution)/shard_map/ppermute | solution.py:20
  115.0 10.4 %collective-permute-start.19 = (f32[64,6,1,128]{3,0,2,1:T(8,128)S(1)}, f32[64,6,1,128]{3,0,2,1:T(8,128)S(1)}, u32[]{:S(2)}, u32[]{:S(2)}) collective-permute-start(f32[64,6,1,128]{3,0,2,1:T(8,128)S(1)} %get-tuple-element.12), channel_id=1, source_target_pairs={{0,4},{4,8},{8,12},{12,16},{16,20},{20,24},{24,28},{1,5},{5,9},{9,... | collective-permute-start | bytes 589832 | tf_op jit(solution)/shard_map/ppermute | solution.py:17
  128.8 6.6 collective-permute-start.20
  136.6 7.6 %collective-permute-start.22 = (f32[64,6,1,128]{3,0,2,1:T(8,128)S(1)}, f32[64,6,1,128]{3,0,2,1:T(8,128)S(1)}, u32[]{:S(2)}, u32[]{:S(2)}) collective-permute-start(f32[64,6,1,128]{3,0,2,1:T(8,128)S(1)} %get-tuple-element.11), channel_id=1, source_target_pairs={{4,0},{8,4},{12,8},{16,12},{20,16},{24,20},{28,24},{5,1},{9,5},{13... | collective-permute-start | bytes 589832 | tf_op jit(solution)/shard_map/ppermute | solution.py:20
  138.5 10.4 %collective-permute-start.23 = (f32[64,6,1,128]{3,0,2,1:T(8,128)S(1)}, f32[64,6,1,128]{3,0,2,1:T(8,128)S(1)}, u32[]{:S(2)}, u32[]{:S(2)}) collective-permute-start(f32[64,6,1,128]{3,0,2,1:T(8,128)S(1)} %get-tuple-element.10), channel_id=1, source_target_pairs={{0,4},{4,8},{8,12},{12,16},{16,20},{20,24},{24,28},{1,5},{5,9},{9,... | collective-permute-start | bytes 589832 | tf_op jit(solution)/shard_map/ppermute | solution.py:17
  152.7 6.6 collective-permute-start.24
  160.4 7.6 %collective-permute-start.26 = (f32[64,6,1,128]{3,0,2,1:T(8,128)S(1)}, f32[64,6,1,128]{3,0,2,1:T(8,128)S(1)}, u32[]{:S(2)}, u32[]{:S(2)}) collective-permute-start(f32[64,6,1,128]{3,0,2,1:T(8,128)S(1)} %get-tuple-element.9), channel_id=1, source_target_pairs={{4,0},{8,4},{12,8},{16,12},{20,16},{24,20},{28,24},{5,1},{9,5},{13... | collective-permute-start | bytes 589832 | tf_op jit(solution)/shard_map/ppermute | solution.py:20
  162.3 10.4 %collective-permute-start.27 = (f32[64,6,1,128]{3,0,2,1:T(8,128)S(1)}, f32[64,6,1,128]{3,0,2,1:T(8,128)S(1)}, u32[]{:S(2)}, u32[]{:S(2)}) collective-permute-start(f32[64,6,1,128]{3,0,2,1:T(8,128)S(1)} %get-tuple-element.8), channel_id=1, source_target_pairs={{0,4},{4,8},{8,12},{12,16},{16,20},{20,24},{24,28},{1,5},{5,9},{9,... | collective-permute-start | bytes 589832 | tf_op jit(solution)/shard_map/ppermute | solution.py:17
  176.1 6.6 collective-permute-start.28
  183.9 7.6 %collective-permute-start.30 = (f32[64,6,1,128]{3,0,2,1:T(8,128)S(1)}, f32[64,6,1,128]{3,0,2,1:T(8,128)S(1)}, u32[]{:S(2)}, u32[]{:S(2)}) collective-permute-start(f32[64,6,1,128]{3,0,2,1:T(8,128)S(1)} %get-tuple-element.7), channel_id=1, source_target_pairs={{4,0},{8,4},{12,8},{16,12},{20,16},{24,20},{28,24},{5,1},{9,5},{13... | collective-permute-start | bytes 589832 | tf_op jit(solution)/shard_map/ppermute | solution.py:20
  185.8 10.4 %collective-permute-start.31 = (f32[64,6,1,128]{3,0,2,1:T(8,128)S(1)}, f32[64,6,1,128]{3,0,2,1:T(8,128)S(1)}, u32[]{:S(2)}, u32[]{:S(2)}) collective-permute-start(f32[64,6,1,128]{3,0,2,1:T(8,128)S(1)} %get-tuple-element.6), channel_id=1, source_target_pairs={{0,4},{4,8},{8,12},{12,16},{16,20},{20,24},{24,28},{1,5},{5,9},{9,... | collective-permute-start | bytes 589832 | tf_op jit(solution)/shard_map/ppermute | solution.py:17
  201.1 541.1 %all-reduce.10.cloned.1.call-start = ((), (), s32[]{:S(2)}) async-start(), calls=%async_computation.1 | async-start | bytes 131072 | tf_op jit(solution)/shard_map/psum | solution.py:96
  (16 other events, 272.6 us)
Sparse Core Ops, SparseCore 0:
  201.2 61.4 all-gather.1
  266.0 476.0 all-reduce.9
where the time goes:
time: 752 us; the launch traced here: 750 us
  waiting for transfers between devices  596 us (79%)
  starting transfers between devices  93.3 us (12%)
  other arithmetic  28.6 us (4%)
  between operations  14.7 us (2%)
  matrix products  11 us (1%)
    psum x1, waiting for transfers between devices, on_device(): gram = lax.psum(gram_part, ('gx', 'gyz')) / total_cells  475 us
    ppermute x16, starting transfers between devices, with_halo(): lax.ppermute(lax.slice_in_dim(block, block.shape[dim] - width, None, axis...  65.6 us
    all_gather x1, waiting for transfers between devices, on_device(): shard_rows = lax.all_gather(filtered, 'band', axis=0, tiled=True)  60.9 us
    ppermute x16, waiting for transfers between devices, with_halo(): lax.ppermute(lax.slice_in_dim(block, block.shape[dim] - width, None, axis...  46.3 us
    ppermute x16, starting transfers between devices, with_halo(): lax.ppermute(lax.slice_in_dim(block, 0, width, axis=dim), axis, backward)  27.6 us
    concatenate x15, other arithmetic, with_halo(): block = jnp.concatenate([low, block, high], axis=dim)  16.2 us
  transfers between devices with their start and end apart: 34, of which 25 were waited for; matrix products, arithmetic and copies ran while one was open for 2% of the time, Pallas kernels for 0%

commit v1 on v0

--- a/solution.py
+++ b/solution.py
@@ -93,7 +93,7 @@
         own_columns, shard_rows, (((0,), (0,)), ((), ())), preferred_element_type=jnp.float32
     )
     gram_part, rotated_flat = (gram_part, rotated_part)
-    gram = lax.psum(gram_part, ("gx", "gyz")) / total_cells
+    gram = lax.psum(lax.psum(gram_part, "gx"), "gyz") / total_cells
     rotated = rotated_flat.reshape(local_slots, size_x, size_y, size_z)
     return (gram, rotated)
 

time: 752 us -> 416 us (0.55)
  waiting for transfers between devices: 596 us -> 259 us
    psum x1 -> x2, waiting for transfers between devices: 475 us -> 138 us  [on_device(): gram = lax.psum(lax.psum(gram_part, 'gx'), 'gyz') / total_cells]
  transfers between devices with their start and end apart: 34 -> 35, of which waited for: 25 -> 26; matrix products, arithmetic and copies ran while one was open for 2% -> 3% of each run, Pallas kernels for 0% -> 0%
where the time goes in v1:
time: 416 us; the launch traced here: 414 us
  waiting for transfers between devices  259 us (62%)
  starting transfers between devices  93.4 us (22%)
  other arithmetic  28.6 us (7%)
  between operations  14.4 us (3%)
  matrix products  11 us (3%)
  local copies, waits for them, and re-layouts  7.04 us (2%)
    psum x2, waiting for transfers between devices, on_device(): gram = lax.psum(lax.psum(gram_part, 'gx'), 'gyz') / total_cells  138 us
    ppermute x16, starting transfers between devices, with_halo(): lax.ppermute(lax.slice_in_dim(block, block.shape[dim] - width, None, axis...  65.6 us
    all_gather x1, waiting for transfers between devices, on_device(): shard_rows = lax.all_gather(filtered, 'band', axis=0, tiled=True)  61.2 us
    ppermute x16, waiting for transfers between devices, with_halo(): lax.ppermute(lax.slice_in_dim(block, block.shape[dim] - width, None, axis...  46.3 us
    ppermute x16, starting transfers between devices, with_halo(): lax.ppermute(lax.slice_in_dim(block, 0, width, axis=dim), axis, backward)  27.6 us
    concatenate x15, other arithmetic, with_halo(): block = jnp.concatenate([low, block, high], axis=dim)  16.2 us
    ppermute x16, waiting for transfers between devices, with_halo(): lax.ppermute(lax.slice_in_dim(block, 0, width, axis=dim), axis, backward)  13.9 us
    select_n x7, other arithmetic, on_device(): current = jnp.where(active, updated, current)  9.57 us
  transfers between devices with their start and end apart: 35, of which 26 were waited for; matrix products, arithmetic and copies ran while one was open for 3% of the time, Pallas kernels for 0%

profile of v1, /device:TPU:8, one launch (start us, length us, event | category | flops | bytes accessed | tf_op | source)
XLA Modules:
  0.0 413.6 jit_solution(10473860137096531873)
XLA Ops:
  21.3 3.7 collective-permute-start.2
  29.3 6.6 %collective-permute-done.3 = f32[64,6,1,128]{3,0,2,1:T(8,128)S(1)} collective-permute-done((f32[64,6,1,128]{3,0,2,1:T(8,128)S(1)}, f32[64,6,1,128]{3,0,2,1:T(8,128)S(1)}, u32[]{:S(2)}, u32[]{:S(2)}) %collective-permute-start.3) | collective-permute-done | bytes 196640 | tf_op jit(solution)/shard_map/ppermute | solution.py:17
  45.5 3.8 collective-permute-start.7
  59.2 4.8 %collective-permute-start.9 = (f32[64,1,8,128]{3,0,2,1:T(8,128)S(1)}, f32[64,1,8,128]{3,0,2,1:T(8,128)S(1)}, u32[]{:S(2)}, u32[]{:S(2)}) collective-permute-start(f32[64,1,8,128]{3,0,2,1:T(8,128)S(1)} %get-tuple-element.32), channel_id=1, source_target_pairs={{0,32},{32,64},{64,96},{96,128},{128,160},{160,192},{192,224},{1,3... | collective-permute-start | bytes 786440 | tf_op jit(solution)/shard_map/ppermute | solution.py:17
  67.1 3.9 collective-permute-start.11
  72.7 4.7 %collective-permute-done.11 = f32[64,6,1,128]{3,0,2,1:T(8,128)S(1)} collective-permute-done((f32[64,6,1,128]{3,0,2,1:T(8,128)S(1)}, f32[64,6,1,128]{3,0,2,1:T(8,128)S(1)}, u32[]{:S(2)}, u32[]{:S(2)}) %collective-permute-start.11) | collective-permute-done | bytes 196640 | tf_op jit(solution)/shard_map/ppermute | solution.py:17
  82.6 5.3 %collective-permute-start.13 = (f32[64,1,8,128]{3,0,2,1:T(8,128)S(1)}, f32[64,1,8,128]{3,0,2,1:T(8,128)S(1)}, u32[]{:S(2)}, u32[]{:S(2)}) collective-permute-start(f32[64,1,8,128]{3,0,2,1:T(8,128)S(1)} %get-tuple-element.30), channel_id=1, source_target_pairs={{0,32},{32,64},{64,96},{96,128},{128,160},{160,192},{192,224},{1,3... | collective-permute-start | bytes 786440 | tf_op jit(solution)/shard_map/ppermute | solution.py:17
  91.0 4.1 collective-permute-start.15
  96.6 4.7 %collective-permute-done.15 = f32[64,6,1,128]{3,0,2,1:T(8,128)S(1)} collective-permute-done((f32[64,6,1,128]{3,0,2,1:T(8,128)S(1)}, f32[64,6,1,128]{3,0,2,1:T(8,128)S(1)}, u32[]{:S(2)}, u32[]{:S(2)}) %collective-permute-start.15) | collective-permute-done | bytes 196640 | tf_op jit(solution)/shard_map/ppermute | solution.py:17
  106.7 5.3 %collective-permute-start.17 = (f32[64,1,8,128]{3,0,2,1:T(8,128)S(1)}, f32[64,1,8,128]{3,0,2,1:T(8,128)S(1)}, u32[]{:S(2)}, u32[]{:S(2)}) collective-permute-start(f32[64,1,8,128]{3,0,2,1:T(8,128)S(1)} %get-tuple-element.28), channel_id=1, source_target_pairs={{0,32},{32,64},{64,96},{96,128},{128,160},{160,192},{192,224},{1,3... | collective-permute-start | bytes 786440 | tf_op jit(solution)/shard_map/ppermute | solution.py:17
  115.0 3.9 collective-permute-start.19
  120.7 4.7 %collective-permute-done.19 = f32[64,6,1,128]{3,0,2,1:T(8,128)S(1)} collective-permute-done((f32[64,6,1,128]{3,0,2,1:T(8,128)S(1)}, f32[64,6,1,128]{3,0,2,1:T(8,128)S(1)}, u32[]{:S(2)}, u32[]{:S(2)}) %collective-permute-start.19) | collective-permute-done | bytes 196640 | tf_op jit(solution)/shard_map/ppermute | solution.py:17
  130.1 5.3 %collective-permute-start.21 = (f32[64,1,8,128]{3,0,2,1:T(8,128)S(1)}, f32[64,1,8,128]{3,0,2,1:T(8,128)S(1)}, u32[]{:S(2)}, u32[]{:S(2)}) collective-permute-start(f32[64,1,8,128]{3,0,2,1:T(8,128)S(1)} %get-tuple-element.26), channel_id=1, source_target_pairs={{0,32},{32,64},{64,96},{96,128},{128,160},{160,192},{192,224},{1,3... | collective-permute-start | bytes 786440 | tf_op jit(solution)/shard_map/ppermute | solution.py:17
  138.5 3.9 collective-permute-start.23
  144.2 4.7 %collective-permute-done.23 = f32[64,6,1,128]{3,0,2,1:T(8,128)S(1)} collective-permute-done((f32[64,6,1,128]{3,0,2,1:T(8,128)S(1)}, f32[64,6,1,128]{3,0,2,1:T(8,128)S(1)}, u32[]{:S(2)}, u32[]{:S(2)}) %collective-permute-start.23) | collective-permute-done | bytes 196640 | tf_op jit(solution)/shard_map/ppermute | solution.py:17
  154.0 5.3 %collective-permute-start.25 = (f32[64,1,8,128]{3,0,2,1:T(8,128)S(1)}, f32[64,1,8,128]{3,0,2,1:T(8,128)S(1)}, u32[]{:S(2)}, u32[]{:S(2)}) collective-permute-start(f32[64,1,8,128]{3,0,2,1:T(8,128)S(1)} %get-tuple-element.24), channel_id=1, source_target_pairs={{0,32},{32,64},{64,96},{96,128},{128,160},{160,192},{192,224},{1,3... | collective-permute-start | bytes 786440 | tf_op jit(solution)/shard_map/ppermute | solution.py:17
  162.3 3.9 collective-permute-start.27
  168.0 4.7 %collective-permute-done.27 = f32[64,6,1,128]{3,0,2,1:T(8,128)S(1)} collective-permute-done((f32[64,6,1,128]{3,0,2,1:T(8,128)S(1)}, f32[64,6,1,128]{3,0,2,1:T(8,128)S(1)}, u32[]{:S(2)}, u32[]{:S(2)}) %collective-permute-start.27) | collective-permute-done | bytes 196640 | tf_op jit(solution)/shard_map/ppermute | solution.py:17
  177.4 5.3 %collective-permute-start.29 = (f32[64,1,8,128]{3,0,2,1:T(8,128)S(1)}, f32[64,1,8,128]{3,0,2,1:T(8,128)S(1)}, u32[]{:S(2)}, u32[]{:S(2)}) collective-permute-start(f32[64,1,8,128]{3,0,2,1:T(8,128)S(1)} %get-tuple-element.22), channel_id=1, source_target_pairs={{0,32},{32,64},{64,96},{96,128},{128,160},{160,192},{192,224},{1,3... | collective-permute-start | bytes 786440 | tf_op jit(solution)/shard_map/ppermute | solution.py:17
  185.8 3.9 collective-permute-start.31
  191.4 4.7 %collective-permute-done.31 = f32[64,6,1,128]{3,0,2,1:T(8,128)S(1)} collective-permute-done((f32[64,6,1,128]{3,0,2,1:T(8,128)S(1)}, f32[64,6,1,128]{3,0,2,1:T(8,128)S(1)}, u32[]{:S(2)}, u32[]{:S(2)}) %collective-permute-start.31) | collective-permute-done | bytes 196640 | tf_op jit(solution)/shard_map/ppermute | solution.py:17
  201.5 61.2 %all-gather.2.cloned.1.call-done = bf16[256,4096]{1,0:T(8,128)(2,1)} async-done(((bf16[64,4096]{1,0:T(8,128)(2,1)}), bf16[256,4096]{1,0:T(8,128)(2,1)}) %all-gather.2.cloned.1.call-update) | async-done | bytes 2097168 | tf_op jit(solution)/shard_map/all_gather | solution.py:87
  266.3 61.7 %all-reduce.11.cloned.1.call-done = f32[64,256]{1,0:T(8,128)} async-done(((f32[64,256]{1,0:T(8,128)}), f32[64,256]{1,0:T(8,128)}) %all-reduce.11.cloned.1.call-update) | async-done | bytes 65552 | tf_op jit(solution)/shard_map/psum | solution.py:96
  329.7 75.9 %all-reduce.13.cloned.1.call-done = f32[64,256]{1,0:T(8,128)} async-done(((f32[64,256]{1,0:T(8,128)}), f32[64,256]{1,0:T(8,128)}) %all-reduce.13.cloned.1.call-update) | async-done | bytes 65552 | tf_op jit(solution)/shard_map/psum | solution.py:96
  (112 shorter events, 102.9 us)
Async XLA Ops:
  7.2 255.5 %all-gather.2.cloned.1.call-start = ((), (), s32[]{:S(2)}) async-start(), calls=%async_computation | async-start | bytes 2621440 | tf_op jit(solution)/shard_map/all_gather | solution.py:87
  9.1 11.5 %collective-permute-start.1 = (f32[64,1,8,128]{3,0,2,1:T(8,128)S(1)}, f32[64,1,8,128]{3,0,2,1:T(8,128)S(1)}, u32[]{:S(2)}, u32[]{:S(2)}) collective-permute-start(f32[64,1,8,128]{3,0,2,1:T(8,128)S(1)} %get-tuple-element.37), channel_id=1, source_target_pairs={{0,32},{32,64},{64,96},{96,128},{128,160},{160,192},{192,224},{1,3... | collective-permute-start | bytes 786440 | tf_op jit(solution)/shard_map/ppermute | solution.py:17
  10.9 10.4 %collective-permute-start = (f32[64,1,8,128]{3,0,2,1:T(8,128)S(1)}, f32[64,1,8,128]{3,0,2,1:T(8,128)S(1)}, u32[]{:S(2)}, u32[]{:S(2)}) collective-permute-start(f32[64,1,8,128]{3,0,2,1:T(8,128)S(1)} %get-tuple-element.36), channel_id=1, source_target_pairs={{32,0},{64,32},{96,64},{128,96},{160,128},{192,160},{224,192},{33,... | collective-permute-start | bytes 786440 | tf_op jit(solution)/shard_map/ppermute | solution.py:20
  21.3 8.0 %collective-permute-start.2 = (f32[64,6,1,128]{3,0,2,1:T(8,128)S(1)}, f32[64,6,1,128]{3,0,2,1:T(8,128)S(1)}, u32[]{:S(2)}, u32[]{:S(2)}) collective-permute-start(f32[64,6,1,128]{3,0,2,1:T(8,128)S(1)} %get-tuple-element.21), channel_id=1, source_target_pairs={{4,0},{8,4},{12,8},{16,12},{20,16},{24,20},{28,24},{5,1},{9,5},{13... | collective-permute-start | bytes 589832 | tf_op jit(solution)/shard_map/ppermute | solution.py:20
  25.1 10.9 %collective-permute-start.3 = (f32[64,6,1,128]{3,0,2,1:T(8,128)S(1)}, f32[64,6,1,128]{3,0,2,1:T(8,128)S(1)}, u32[]{:S(2)}, u32[]{:S(2)}) collective-permute-start(f32[64,6,1,128]{3,0,2,1:T(8,128)S(1)} %get-tuple-element.20), channel_id=1, source_target_pairs={{0,4},{4,8},{8,12},{12,16},{16,20},{20,24},{24,28},{1,5},{5,9},{9,... | collective-permute-start | bytes 589832 | tf_op jit(solution)/shard_map/ppermute | solution.py:17
  43.4 7.6 %collective-permute-start.6 = (f32[64,6,1,128]{3,0,2,1:T(8,128)S(1)}, f32[64,6,1,128]{3,0,2,1:T(8,128)S(1)}, u32[]{:S(2)}, u32[]{:S(2)}) collective-permute-start(f32[64,6,1,128]{3,0,2,1:T(8,128)S(1)} %get-tuple-element.19), channel_id=1, source_target_pairs={{4,0},{8,4},{12,8},{16,12},{20,16},{24,20},{28,24},{5,1},{9,5},{13... | collective-permute-start | bytes 589832 | tf_op jit(solution)/shard_map/ppermute | solution.py:20
  45.5 9.0 %collective-permute-start.7 = (f32[64,6,1,128]{3,0,2,1:T(8,128)S(1)}, f32[64,6,1,128]{3,0,2,1:T(8,128)S(1)}, u32[]{:S(2)}, u32[]{:S(2)}) collective-permute-start(f32[64,6,1,128]{3,0,2,1:T(8,128)S(1)} %get-tuple-element.18), channel_id=1, source_target_pairs={{0,4},{4,8},{8,12},{12,16},{16,20},{20,24},{24,28},{1,5},{5,9},{9,... | collective-permute-start | bytes 589832 | tf_op jit(solution)/shard_map/ppermute | solution.py:17
  65.1 7.6 %collective-permute-start.10 = (f32[64,6,1,128]{3,0,2,1:T(8,128)S(1)}, f32[64,6,1,128]{3,0,2,1:T(8,128)S(1)}, u32[]{:S(2)}, u32[]{:S(2)}) collective-permute-start(f32[64,6,1,128]{3,0,2,1:T(8,128)S(1)} %get-tuple-element.17), channel_id=1, source_target_pairs={{4,0},{8,4},{12,8},{16,12},{20,16},{24,20},{28,24},{5,1},{9,5},{13... | collective-permute-start | bytes 589832 | tf_op jit(solution)/shard_map/ppermute | solution.py:20
  67.1 10.4 %collective-permute-start.11 = (f32[64,6,1,128]{3,0,2,1:T(8,128)S(1)}, f32[64,6,1,128]{3,0,2,1:T(8,128)S(1)}, u32[]{:S(2)}, u32[]{:S(2)}) collective-permute-start(f32[64,6,1,128]{3,0,2,1:T(8,128)S(1)} %get-tuple-element.16), channel_id=1, source_target_pairs={{0,4},{4,8},{8,12},{12,16},{16,20},{20,24},{24,28},{1,5},{5,9},{9,... | collective-permute-start | bytes 589832 | tf_op jit(solution)/shard_map/ppermute | solution.py:17
  81.3 6.6 %collective-permute-start.12 = (f32[64,1,8,128]{3,0,2,1:T(8,128)S(1)}, f32[64,1,8,128]{3,0,2,1:T(8,128)S(1)}, u32[]{:S(2)}, u32[]{:S(2)}) collective-permute-start(f32[64,1,8,128]{3,0,2,1:T(8,128)S(1)} %get-tuple-element.31), channel_id=1, source_target_pairs={{32,0},{64,32},{96,64},{128,96},{160,128},{192,160},{224,192},{33,... | collective-permute-start | bytes 786440 | tf_op jit(solution)/shard_map/ppermute | solution.py:20
  89.0 7.6 %collective-permute-start.14 = (f32[64,6,1,128]{3,0,2,1:T(8,128)S(1)}, f32[64,6,1,128]{3,0,2,1:T(8,128)S(1)}, u32[]{:S(2)}, u32[]{:S(2)}) collective-permute-start(f32[64,6,1,128]{3,0,2,1:T(8,128)S(1)} %get-tuple-element.15), channel_id=1, source_target_pairs={{4,0},{8,4},{12,8},{16,12},{20,16},{24,20},{28,24},{5,1},{9,5},{13... | collective-permute-start | bytes 589832 | tf_op jit(solution)/shard_map/ppermute | solution.py:20
  91.0 10.4 %collective-permute-start.15 = (f32[64,6,1,128]{3,0,2,1:T(8,128)S(1)}, f32[64,6,1,128]{3,0,2,1:T(8,128)S(1)}, u32[]{:S(2)}, u32[]{:S(2)}) collective-permute-start(f32[64,6,1,128]{3,0,2,1:T(8,128)S(1)} %get-tuple-element.14), channel_id=1, source_target_pairs={{0,4},{4,8},{8,12},{12,16},{16,20},{20,24},{24,28},{1,5},{5,9},{9,... | collective-permute-start | bytes 589832 | tf_op jit(solution)/shard_map/ppermute | solution.py:17
  113.1 7.6 %collective-permute-start.18 = (f32[64,6,1,128]{3,0,2,1:T(8,128)S(1)}, f32[64,6,1,128]{3,0,2,1:T(8,128)S(1)}, u32[]{:S(2)}, u32[]{:S(2)}) collective-permute-start(f32[64,6,1,128]{3,0,2,1:T(8,128)S(1)} %get-tuple-element.13), channel_id=1, source_target_pairs={{4,0},{8,4},{12,8},{16,12},{20,16},{24,20},{28,24},{5,1},{9,5},{13... | collective-permute-start | bytes 589832 | tf_op jit(solution)/shard_map/ppermute | solution.py:20
  115.0 10.4 %collective-permute-start.19 = (f32[64,6,1,128]{3,0,2,1:T(8,128)S(1)}, f32[64,6,1,128]{3,0,2,1:T(8,128)S(1)}, u32[]{:S(2)}, u32[]{:S(2)}) collective-permute-start(f32[64,6,1,128]{3,0,2,1:T(8,128)S(1)} %get-tuple-element.12), channel_id=1, source_target_pairs={{0,4},{4,8},{8,12},{12,16},{16,20},{20,24},{24,28},{1,5},{5,9},{9,... | collective-permute-start | bytes 589832 | tf_op jit(solution)/shard_map/ppermute | solution.py:17
  128.8 6.6 %collective-permute-start.20 = (f32[64,1,8,128]{3,0,2,1:T(8,128)S(1)}, f32[64,1,8,128]{3,0,2,1:T(8,128)S(1)}, u32[]{:S(2)}, u32[]{:S(2)}) collective-permute-start(f32[64,1,8,128]{3,0,2,1:T(8,128)S(1)} %get-tuple-element.27), channel_id=1, source_target_pairs={{32,0},{64,32},{96,64},{128,96},{160,128},{192,160},{224,192},{33,... | collective-permute-start | bytes 786440 | tf_op jit(solution)/shard_map/ppermute | solution.py:20
  136.6 7.6 %collective-permute-start.22 = (f32[64,6,1,128]{3,0,2,1:T(8,128)S(1)}, f32[64,6,1,128]{3,0,2,1:T(8,128)S(1)}, u32[]{:S(2)}, u32[]{:S(2)}) collective-permute-start(f32[64,6,1,128]{3,0,2,1:T(8,128)S(1)} %get-tuple-element.11), channel_id=1, source_target_pairs={{4,0},{8,4},{12,8},{16,12},{20,16},{24,20},{28,24},{5,1},{9,5},{13... | collective-permute-start | bytes 589832 | tf_op jit(solution)/shard_map/ppermute | solution.py:20
  138.5 10.4 %collective-permute-start.23 = (f32[64,6,1,128]{3,0,2,1:T(8,128)S(1)}, f32[64,6,1,128]{3,0,2,1:T(8,128)S(1)}, u32[]{:S(2)}, u32[]{:S(2)}) collective-permute-start(f32[64,6,1,128]{3,0,2,1:T(8,128)S(1)} %get-tuple-element.10), channel_id=1, source_target_pairs={{0,4},{4,8},{8,12},{12,16},{16,20},{20,24},{24,28},{1,5},{5,9},{9,... | collective-permute-start | bytes 589832 | tf_op jit(solution)/shard_map/ppermute | solution.py:17
  152.7 6.6 %collective-permute-start.24 = (f32[64,1,8,128]{3,0,2,1:T(8,128)S(1)}, f32[64,1,8,128]{3,0,2,1:T(8,128)S(1)}, u32[]{:S(2)}, u32[]{:S(2)}) collective-permute-start(f32[64,1,8,128]{3,0,2,1:T(8,128)S(1)} %get-tuple-element.25), channel_id=1, source_target_pairs={{32,0},{64,32},{96,64},{128,96},{160,128},{192,160},{224,192},{33,... | collective-permute-start | bytes 786440 | tf_op jit(solution)/shard_map/ppermute | solution.py:20
  160.4 7.6 %collective-permute-start.26 = (f32[64,6,1,128]{3,0,2,1:T(8,128)S(1)}, f32[64,6,1,128]{3,0,2,1:T(8,128)S(1)}, u32[]{:S(2)}, u32[]{:S(2)}) collective-permute-start(f32[64,6,1,128]{3,0,2,1:T(8,128)S(1)} %get-tuple-element.9), channel_id=1, source_target_pairs={{4,0},{8,4},{12,8},{16,12},{20,16},{24,20},{28,24},{5,1},{9,5},{13... | collective-permute-start | bytes 589832 | tf_op jit(solution)/shard_map/ppermute | solution.py:20
  162.3 10.4 %collective-permute-start.27 = (f32[64,6,1,128]{3,0,2,1:T(8,128)S(1)}, f32[64,6,1,128]{3,0,2,1:T(8,128)S(1)}, u32[]{:S(2)}, u32[]{:S(2)}) collective-permute-start(f32[64,6,1,128]{3,0,2,1:T(8,128)S(1)} %get-tuple-element.8), channel_id=1, source_target_pairs={{0,4},{4,8},{8,12},{12,16},{16,20},{20,24},{24,28},{1,5},{5,9},{9,... | collective-permute-start | bytes 589832 | tf_op jit(solution)/shard_map/ppermute | solution.py:17
  183.9 7.6 %collective-permute-start.30 = (f32[64,6,1,128]{3,0,2,1:T(8,128)S(1)}, f32[64,6,1,128]{3,0,2,1:T(8,128)S(1)}, u32[]{:S(2)}, u32[]{:S(2)}) collective-permute-start(f32[64,6,1,128]{3,0,2,1:T(8,128)S(1)} %get-tuple-element.7), channel_id=1, source_target_pairs={{4,0},{8,4},{12,8},{16,12},{20,16},{24,20},{28,24},{5,1},{9,5},{13... | collective-permute-start | bytes 589832 | tf_op jit(solution)/shard_map/ppermute | solution.py:20
  185.8 10.4 %collective-permute-start.31 = (f32[64,6,1,128]{3,0,2,1:T(8,128)S(1)}, f32[64,6,1,128]{3,0,2,1:T(8,128)S(1)}, u32[]{:S(2)}, u32[]{:S(2)}) collective-permute-start(f32[64,6,1,128]{3,0,2,1:T(8,128)S(1)} %get-tuple-element.6), channel_id=1, source_target_pairs={{0,4},{4,8},{8,12},{12,16},{16,20},{20,24},{24,28},{1,5},{5,9},{9,... | collective-permute-start | bytes 589832 | tf_op jit(solution)/shard_map/ppermute | solution.py:17
  201.1 126.9 %all-reduce.11.cloned.1.call-start = ((), (), s32[]{:S(2)}) async-start(), calls=%async_computation.1 | async-start | bytes 131072 | tf_op jit(solution)/shard_map/psum | solution.py:96
  265.9 139.7 %all-reduce.13.cloned.1.call-start = ((), (), s32[]{:S(2)}) async-start(), calls=%async_computation.2 | async-start | bytes 131072 | tf_op jit(solution)/shard_map/psum | solution.py:96
  (17 other events, 341.3 us)
Sparse Core Ops, SparseCore 0:
  201.2 61.4 all-gather.1
  266.0 61.9 all-reduce.10
  330.8 74.7 all-reduce.12
